TPU v7x, 128 devices: a whole 4x4x4 slice. The times are simulated.
128 devices in a mesh: dp: 32 (over y, x, z_lo), tensor: 4 (over z_hi, core).
Axes of the slice: x: 4, y: 4, z: 4 (z_hi: 2, z_lo: 2; z = z_hi * 2 + z_lo), core: 2. Of those that a mesh axis runs over, the one named last changes fastest.
Arguments:
- activations: bfloat16 [2, 65536, 4096], P(None, 'dp', 'tensor'), may hold values from -6 to 6
- out_grads: bfloat16 [2, 65536, 4096], P(None, 'dp', 'tensor'), may hold values from -6 to 6
- proj_in: bfloat16 [2, 4096, 16], P(None, 'tensor'), may hold values from -0.09375 to 0.09375
- proj_out: bfloat16 [2, 4096, 16], P(None, 'tensor'), may hold values from -0.09375 to 0.09375
- lengths: int32 [1024], P('dp'), may hold values from 16 to 64
- queries: float32 [512, 512], P('dp', 'tensor'), may hold values from -6 to 6
Outputs:
- scores: float32 [1024, 512], P('dp', 'tensor')
All inputs are finite; a program needn't handle non-finite values.
Results may differ from a plain program's by a relative error of at most 0.028.
Values may be sent and summed in bfloat16 or wider, within the bound.
A program may use at most 64 MiB of HBM per device.

v0:
```python
import math

import jax
import jax.numpy as jnp
from jax import lax
from jax.sharding import PartitionSpec as P

ITERS = 4


DAMPING = 0.1


def on_device(activations, out_grads, proj_in, proj_out, lengths, queries):
    linears, tok_dev, feature_shard = activations.shape
    seq_dev = lengths.shape[0]
    seq_len = tok_dev // seq_dev
    rank_dim = proj_in.shape[2]
    inner_proj = jnp.einsum(
        "ltd,ldr->ltr", activations, proj_in, preferred_element_type=jnp.float32
    )
    outer_proj = jnp.einsum("ltd,ldr->ltr", out_grads, proj_out, preferred_element_type=jnp.float32)
    inner_proj, outer_proj = lax.psum((inner_proj, outer_proj), "tensor")
    live_tokens = (jnp.arange(seq_len)[None, :] < lengths[:, None]).astype(jnp.float32)
    inner_proj = inner_proj.reshape(linears, seq_dev, seq_len, rank_dim)
    outer_proj = (
        outer_proj.reshape(linears, seq_dev, seq_len, rank_dim) * live_tokens[None, :, :, None]
    )
    seq_blocks = jnp.einsum("lsta,lstb->slab", outer_proj, inner_proj) / math.sqrt(seq_len)
    vectors = seq_blocks.reshape(seq_dev, linears * rank_dim * rank_dim).astype(jnp.bfloat16)
    vec_dim = vectors.shape[1]
    total_seqs = seq_dev * lax.axis_size("dp")
    gram_rows = lax.psum_scatter(
        jnp.einsum("sk,sj->kj", vectors, vectors, preferred_element_type=jnp.float32),
        "dp",
        scatter_dimension=0,
        tiled=True,
    )
    gram_rows = gram_rows / total_seqs

    def column_norm(residual):
        return lax.psum(jnp.sum(residual * residual, axis=0), "dp")

    solution = jnp.zeros_like(queries)
    residual = queries
    direction = queries
    norm_now = column_norm(residual)
    for iteration in range(ITERS):
        operator_image = jnp.dot(
            gram_rows,
            lax.all_gather(direction, "dp", axis=0, tiled=True),
            precision=lax.Precision.HIGHEST,
            preferred_element_type=jnp.float32,
        )
        operator_image = operator_image + DAMPING * direction
        curvature = lax.psum(jnp.sum(direction * operator_image, axis=0), "dp")
        step_size = norm_now / curvature
        solution = solution + step_size * direction
        residual = residual - step_size * operator_image
        norm_next = column_norm(residual)
        direction = residual + norm_next / norm_now * direction
        norm_now = norm_next
    solution_bf = solution.astype(jnp.bfloat16)
    scores = jnp.dot(
        vectors,
        lax.all_gather(solution_bf, "dp", axis=0, tiled=True),
        preferred_element_type=jnp.float32,
    )
    return scores / math.sqrt(vec_dim)


def solution(mesh):
    placed = (
        P(None, "dp", "tensor"),
        P(None, "dp", "tensor"),
        P(None, "tensor", None),
        P(None, "tensor", None),
        P("dp"),
        P("dp", "tensor"),
    )
    return jax.shard_map(
        on_device, mesh=mesh, in_specs=placed, out_specs=P("dp", "tensor"), check_vma=False
    )
```

profile of v0, /device:TPU:0, one launch (start us, length us, event | category | flops | bytes accessed | tf_op | source)
XLA Modules:
  0.0 1090.1 jit_solution(14680329260902168836)
XLA Ops:
  7.4 5.7 fusion.18
  13.3 1.1 copy.9
  14.5 5.7 fusion.19
  20.8 23.0 %all-reduce.5 = bf16[2,32,64,16]{2,3,0,1:T(8,128)(2,1)S(1)} all-reduce(f32[2,32,64,16]{2,3,0,1:T(8,128)S(1)} %copy.10), channel_id=1, replica_groups=mesh['dp'=32,'tensor'=4] {'tensor'}, use_global_device_ids=true, to_apply=%region_1.0 | all-reduce | flops 65536 | bytes 393216 | tf_op jit(solution)/shard_map/psum | solution.py:23
  43.8 16.6 %all-reduce.4.cloned.1.call-done = f32[2,32,64,16]{2,3,0,1:T(8,128)} async-done(((f32[2,32,64,16]{2,3,0,1:T(8,128)}), f32[2,32,64,16]{2,3,0,1:T(8,128)}) %all-reduce.4.cloned.1.call-update) | async-done | bytes 262160 | tf_op jit(solution)/shard_map/psum | solution.py:23
  60.4 1.3 fusion
  62.0 1.3 fusion.20
  63.3 82.0 %all_gather.15 = f32[512,128]{1,0:T(8,128)S(1)} all-gather(f32[16,128]{1,0:T(8,128)S(1)} %copy-done.1), channel_id=1, replica_groups=mesh['dp'=32,'tensor'=4] {'dp'}, dimensions={0}, use_global_device_ids=true | all-gather | bytes 270336 | tf_op jit(solution)/shard_map/all_gather | solution.py:51
  145.3 78.7 %reduce-scatter.2.cloned.1.call-done = f32[16,512]{1,0:T(8,128)} async-done(((f32[512,512]{1,0:T(8,128)}), f32[16,512]{1,0:T(8,128)}) %reduce-scatter.2.cloned.1.call-update) | async-done | bytes 32784 | tf_op jit(solution)/shard_map/reduce_scatter | solution.py:33
  224.0 1.0 multiply_reduce_fusion.5
  225.0 77.4 %all-reduce = (f32[128]{0:T(128)S(1)}, f32[128]{0:T(128)S(1)}) all-reduce(f32[128]{0:T(128)S(1)} %get-tuple-element.6, f32[128]{0:T(128)S(1)} %get-tuple-element.5), channel_id=1, replica_groups=mesh['dp'=32,'tensor'=4] {'dp'}, use_global_device_ids=true, to_apply=%region_3.0 | all-reduce | flops 256 | bytes 2048 | tf_op jit(solution)/shard_map/psum | solution.py:42
  302.5 78.3 %psum.74 = f32[128]{0:T(128)S(1)} all-reduce(f32[128]{0:T(128)S(1)} %multiply_reduce_fusion.4), channel_id=1, replica_groups=mesh['dp'=32,'tensor'=4] {'dp'}, use_global_device_ids=true, to_apply=%region_8.0 | all-reduce | flops 128 | bytes 1024 | tf_op jit(solution)/shard_map/psum | solution.py:42
  380.8 77.2 %all_gather.16 = f32[512,128]{1,0:T(8,128)S(1)} all-gather(f32[16,128]{1,0:T(8,128)S(1)} %multiply_add_fusion.2), channel_id=1, replica_groups=mesh['dp'=32,'tensor'=4] {'dp'}, dimensions={0}, use_global_device_ids=true | all-gather | bytes 270336 | tf_op jit(solution)/shard_map/all_gather | solution.py:51
  458.0 1.0 multiply_reduce_fusion.3
  459.0 78.3 %psum.75 = f32[128]{0:T(128)S(1)} all-reduce(f32[128]{0:T(128)S(1)} %get-tuple-element.12), channel_id=1, replica_groups=mesh['dp'=32,'tensor'=4] {'dp'}, use_global_device_ids=true, to_apply=%region_10.0 | all-reduce | flops 128 | bytes 1024 | tf_op jit(solution)/shard_map/psum | solution.py:56
  537.3 77.4 %psum.76 = f32[128]{0:T(128)S(1)} all-reduce(f32[128]{0:T(128)S(1)} %get-tuple-element.9), channel_id=1, replica_groups=mesh['dp'=32,'tensor'=4] {'dp'}, use_global_device_ids=true, to_apply=%region_12.0 | all-reduce | flops 128 | bytes 1024 | tf_op jit(solution)/shard_map/psum | solution.py:42
  614.7 78.2 %all_gather.17 = f32[512,128]{1,0:T(8,128)S(1)} all-gather(f32[16,128]{1,0:T(8,128)S(1)} %multiply_add_fusion.1), channel_id=1, replica_groups=mesh['dp'=32,'tensor'=4] {'dp'}, dimensions={0}, use_global_device_ids=true | all-gather | bytes 270336 | tf_op jit(solution)/shard_map/all_gather | solution.py:51
  692.8 1.0 multiply_reduce_fusion.1
  693.9 77.3 %psum.77 = f32[128]{0:T(128)S(1)} all-reduce(f32[128]{0:T(128)S(1)} %get-tuple-element.14), channel_id=1, replica_groups=mesh['dp'=32,'tensor'=4] {'dp'}, use_global_device_ids=true, to_apply=%region_14.0 | all-reduce | flops 128 | bytes 1024 | tf_op jit(solution)/shard_map/psum | solution.py:56
  771.2 78.4 %psum.78 = f32[128]{0:T(128)S(1)} all-reduce(f32[128]{0:T(128)S(1)} %multiply_reduce_fusion), channel_id=1, replica_groups=mesh['dp'=32,'tensor'=4] {'dp'}, use_global_device_ids=true, to_apply=%region_16.0 | all-reduce | flops 128 | bytes 1024 | tf_op jit(solution)/shard_map/psum | solution.py:42
  849.6 77.1 %all_gather.18 = f32[512,128]{1,0:T(8,128)S(1)} all-gather(f32[16,128]{1,0:T(8,128)S(1)} %multiply_add_fusion), channel_id=1, replica_groups=mesh['dp'=32,'tensor'=4] {'dp'}, dimensions={0}, use_global_device_ids=true | all-gather | bytes 270336 | tf_op jit(solution)/shard_map/all_gather | solution.py:51
  926.7 1.0 fusion.2
  927.7 78.4 %psum.79 = f32[128]{0:T(128)S(1)} all-reduce(f32[128]{0:T(128)S(1)} %fusion.2), channel_id=1, replica_groups=mesh['dp'=32,'tensor'=4] {'dp'}, use_global_device_ids=true, to_apply=%region_18.0 | all-reduce | flops 128 | bytes 1024 | tf_op jit(solution)/shard_map/psum | solution.py:56
  1006.1 76.3 %all_gather.19 = bf16[512,128]{1,0:T(8,128)(2,1)S(1)} all-gather(bf16[16,128]{1,0:T(8,128)(2,1)S(1)} %add_convert_fusion), channel_id=1, replica_groups=mesh['dp'=32,'tensor'=4] {'dp'}, dimensions={0}, use_global_device_ids=true | all-gather | bytes 135168 | tf_op jit(solution)/shard_map/all_gather | solution.py:66
  (32 shorter events, 3.1 us)
Async XLA Ops:
  6.5 0.8 copy-start
  6.5 7.9 copy-start.2
  6.5 53.8 %all-reduce.4.cloned.1.call-start = ((), (), s32[]{:S(2)}) async-start(), calls=%async_computation.1 | async-start | bytes 1048576 | tf_op jit(solution)/shard_map/psum | solution.py:23
  13.0 7.7 copy-start.3
  13.3 50.1 %copy-start.1 = (f32[16,128]{1,0:T(8,128)S(1)}, f32[16,128]{1,0:T(8,128)}, u32[]{:S(2)}) copy-start(f32[16,128]{1,0:T(8,128)} %param.11) | copy-start | bytes 24580
  14.4 209.6 %reduce-scatter.2.cloned.1.call-start = ((), (), s32[]{:S(2)}) async-start(), calls=%async_computation.2 | async-start | bytes 1081344 | tf_op jit(solution)/shard_map/reduce_scatter | solution.py:33
Sparse Core Ops, SparseCore 0:
  14.5 45.7 all-reduce.3
  63.4 160.5 reduce-scatter.1
where the time goes:
time: 1090 us
  blocking collectives  959 us (88%)
  waiting for transfers between devices  95.3 us (9%)
  matrix products  18.7 us (2%)
  between operations  13.5 us (1%)
    all_gather x4, blocking collectives, on_device(): lax.all_gather(direction, 'dp', axis=0, tiled=True)  314 us
    psum x4, blocking collectives, column_norm(): return lax.psum(jnp.sum(residual * residual, axis=0), 'dp')  311 us
    psum x3, blocking collectives, on_device(): curvature = lax.psum(jnp.sum(direction * operator_image, axis=0), 'dp')  234 us
    reduce_scatter x1, waiting for transfers between devices, on_device(): lax.psum_scatter(jnp.einsum('sk,sj->kj', vectors, vectors, preferred_elem...  78.7 us
    all_gather x1, blocking collectives, on_device(): lax.all_gather(solution_bf, 'dp', axis=0, tiled=True)  76.3 us
    psum x1, blocking collectives, on_device(): inner_proj, outer_proj = lax.psum((inner_proj, outer_proj), 'tensor')  23 us
  transfers between devices with their start and end apart: 2, of which 2 were waited for; matrix products, arithmetic and copies ran while one was open for 1% of the time, Pallas kernels for 0%

commit v1 on v0

v1 whole, which is shorter than its diff:
```python
import functools
import math

import jax
import jax.numpy as jnp
from jax import lax
from jax.experimental import pallas as pl
from jax.experimental.pallas import tpu as pltpu
from jax.sharding import PartitionSpec as P

ITERS = 4
DAMPING = 0.1
MESH = pl.DeviceIdType.MESH
BF = jnp.bfloat16
F32 = jnp.float32

HOPS = lambda o: sum(min(v, 4 - v) for v in o)
OFFSETS = sorted(
    [(a, b, c) for a in range(4) for b in range(4) for c in range(4)], key=HOPS, reverse=True
)
SELF = len(OFFSETS) - 1
ACROSS = OFFSETS.index((0, 0, 2))
GROUPS = 4
PER_GROUP = len(OFFSETS) // GROUPS
SUB = 2


def split(v):
    hi = v.astype(BF)
    return hi, (v - hi.astype(F32)).astype(BF)


def tn_dot(a, b):
    return lax.dot_general(a, b, (((0,), (0,)), ((), ())), preferred_element_type=F32)


def kernel(
    act, grad, pin, pout, lengths, queries, out,
    abuf, gbuf, pbuf, w, send, part, vsend, own, oth, qbuf, lens, expand,
    in_sem, p_sem, q_sem, l_sem, rs_send, rs_recv, q_send, q_recv, v_send, v_recv, f_send, f_recv,
):
    dp, tensor = lax.axis_index("dp"), lax.axis_index("tensor")
    x, y = lax.rem(dp // 2, 4), dp // 8
    zh, core = tensor // 2, lax.rem(tensor, 2)
    z = zh * 2 + lax.rem(dp, 2)

    def chip(o, other=0):
        tx, ty, tz = (lax.rem(v + d, 4) for v, d in zip((x, y, z), o))
        tc = 1 - core if other else core
        return ((ty * 4 + tx) * 2 + lax.rem(tz, 2), (tz // 2) * 2 + tc)

    sibling = chip((0, 0, 0), 1)
    shares = ((0, 1), (1, 1), (1, 0), (0, 0))
    targets = (chip((0, 0, 2)), chip((0, 0, 2), 1), sibling)
    step = 1024 // SUB

    def load(k, s, which):
        rel, far = shares[k]
        linear = 1 - core if rel else core
        half = 1 - zh if far else zh
        src, dst = ((act, abuf), (grad, gbuf))[which]
        return pltpu.make_async_copy(
            src.at[linear, pl.ds(half * 1024 + s * step, step)],
            dst.at[k, pl.ds(s * step, step)],
            in_sem.at[k, s, which],
        )

    weights = [
        pltpu.make_async_copy(p.at[1 - core if rel else core], pbuf.at[io, rel], p_sem.at[io, rel])
        for io, p in enumerate((pin, pout)) for rel in range(2)
    ]
    for c in weights:
        c.start()
    for k in range(4):
        for s in range(SUB):
            for which in range(2):
                load(k, s, which).start()
    len_copy = pltpu.make_async_copy(lengths, lens, l_sem)
    len_copy.start()
    q_slot = lax.rem(dp + 16 * core, 32)
    q_copy = pltpu.make_async_copy(queries, qbuf.at[q_slot], q_sem)
    q_copy.start()

    barrier = pltpu.get_barrier_semaphore()
    for o in OFFSETS[:SELF]:
        pl.semaphore_signal(barrier, inc=1, device_id=chip(o), device_id_type=MESH)
    for t in targets[1:]:
        pl.semaphore_signal(barrier, inc=1, device_id=t, device_id_type=MESH)

    row = lax.rem(lax.broadcasted_iota(jnp.int32, (256, 256), 0), 128)
    col = lax.broadcasted_iota(jnp.int32, (256, 256), 1)
    for q in range(4):
        expand[q, 0] = jnp.where(row == 32 * q + lax.rem(col, 16), 1.0, 0.0).astype(BF)
        expand[q, 1] = jnp.where(row == 32 * q + 16 + col // 16, 1.0, 0.0).astype(BF)

    for c in weights:
        c.wait()
    zero = jnp.zeros((16, 1024), BF)
    for rel in range(2):
        w[0, rel] = jnp.concatenate([pbuf[0, rel], zero] * 4, axis=0).T
        w[1, rel] = jnp.concatenate([zero, pbuf[1, rel]] * 4, axis=0).T

    lane = lax.broadcasted_iota(jnp.int32, (256, 128), 1)
    token = lax.broadcasted_iota(jnp.int32, (256, 128), 0)
    quarter = lane // 32

    def project(k):
        rel = shares[k][0]
        total = None
        for q in range(4):
            if q % (4 // SUB) == 0:
                for which in range(2):
                    load(k, q // (4 // SUB), which).wait()
            rows = pl.ds(q * 256, 256)
            r = jnp.dot(abuf[k, rows], w[0, rel], preferred_element_type=F32)
            r = r + jnp.dot(gbuf[k, rows], w[1, rel], preferred_element_type=F32)
            total = r if total is None else jnp.where(quarter == q, r, total)
        return total

    def scatter(k):
        return pltpu.make_async_remote_copy(
            src_ref=send.at[k], dst_ref=part.at[k], send_sem=rs_send.at[k], recv_sem=rs_recv.at[k],
            device_id=targets[k], device_id_type=MESH,
        )

    def query_copy(o, low):
        tx, ty = lax.rem(x + o[0], 4), lax.rem(y + o[1], 4)
        tl = lax.rem(lax.rem(dp, 2) + low, 2)
        return pltpu.make_async_remote_copy(
            src_ref=queries, dst_ref=qbuf.at[q_slot], send_sem=q_send, recv_sem=q_recv,
            device_id=((ty * 4 + tx) * 2 + tl, tensor), device_id_type=MESH,
        )

    plane = [(a, b, l) for a in range(4) for b in range(4) for l in range(2) if a or b or l]

    send[0] = project(0).astype(BF)
    pl.semaphore_wait(barrier, SELF + 2)
    scatter(0).start()
    send[1] = project(1).astype(BF)
    scatter(1).start()
    for a, b, l in plane:
        query_copy((a, b), l).start()
    send[2] = project(2).astype(BF)
    scatter(2).start()
    total = project(3)

    len_copy.wait()
    blocks = []
    for rb in range(4):
        n = jnp.zeros((1, 128), jnp.int32)
        for q in range(4):
            n = jnp.where(quarter[:1] == q, lens[zh * 16 + 4 * q + rb], n)
        n = jnp.where(lax.rem(lane[:1], 32) < 16, 64, n)
        blocks.append(jnp.broadcast_to(n, (64, 128)))
    live = lax.rem(token, 64) < jnp.concatenate(blocks, axis=0)

    for k in (2, 0, 1):
        scatter(k).wait_recv()
        total = total + part[k].astype(F32)
    total = jnp.where(live, total, 0.0)
    both = jnp.concatenate(split(total), axis=1)
    rows = []
    for q in range(4):
        inner = jnp.dot(both, expand[q, 0], preferred_element_type=F32)
        outer = jnp.dot(both, expand[q, 1], preferred_element_type=F32)
        prod = outer * inner
        for rb in range(4):
            rows.append(jnp.sum(prod[rb * 64:(rb + 1) * 64], axis=0, keepdims=True))
    vec = (jnp.concatenate(rows, axis=0) * (1.0 / math.sqrt(64))).astype(BF)
    own[SELF] = vec

    def spread(k):
        return pltpu.make_async_remote_copy(
            src_ref=own.at[SELF], dst_ref=own.at[k], send_sem=v_send, recv_sem=v_recv.at[k // PER_GROUP],
            device_id=chip(OFFSETS[k]), device_id_type=MESH,
        )

    for k in range(SELF):
        spread(k).start()

    def group(g):
        return pl.ds(g * PER_GROUP, PER_GROUP)

    def forward(g):
        return pltpu.make_async_remote_copy(
            src_ref=own.at[group(g)], dst_ref=oth.at[group(g)], send_sem=f_send.at[g], recv_sem=f_recv.at[g],
            device_id=sibling, device_id_type=MESH,
        )

    for g in range(GROUPS):
        got = pl.ds(g * PER_GROUP, min(PER_GROUP, SELF - g * PER_GROUP))
        pltpu.make_async_copy(own.at[got], own.at[got], v_recv.at[g]).wait()
        forward(g).start()
    gram = jnp.zeros((512, 512), F32)
    for g in range(GROUPS):
        forward(g).wait_recv()
        vecs = jnp.concatenate(
            [own[group(g)].reshape(256, 256), oth[group(g)].reshape(256, 256)], axis=1
        )
        gram = gram + tn_dot(vecs, vecs)
    gram = gram * (1.0 / 1024)
    g_hi, g_lo = split(gram)

    q_copy.wait()
    others = pl.ds(0, 31)
    pltpu.make_async_copy(qbuf.at[others], qbuf.at[others], q_recv).wait()
    residual = qbuf[...].reshape(512, 128)
    direction = residual
    solution = jnp.zeros_like(residual)
    norm_now = jnp.sum(residual * residual, axis=0, keepdims=True)
    for it in range(ITERS):
        d_hi, d_lo = split(direction)
        wide = jnp.dot(g_hi, jnp.concatenate([d_hi, d_lo], axis=1), preferred_element_type=F32)
        image = wide[:, :128] + wide[:, 128:] + jnp.dot(g_lo, d_hi, preferred_element_type=F32)
        image = image + DAMPING * direction
        step_size = norm_now / jnp.sum(direction * image, axis=0, keepdims=True)
        solution = solution + step_size * direction
        if it < ITERS - 1:
            residual = residual - step_size * image
            norm_next = jnp.sum(residual * residual, axis=0, keepdims=True)
            direction = residual + norm_next / norm_now * direction
            norm_now = norm_next
    solution = solution.astype(BF)
    scale = 1.0 / math.sqrt(512)
    for slot, half in ((SELF, zh), (ACROSS, 1 - zh)):
        v = jnp.concatenate([own[slot], oth[slot]], axis=1)
        out[pl.ds(half * 16, 16)] = jnp.dot(v, solution, preferred_element_type=F32) * scale

    for k in range(3):
        scatter(k).wait_send()
    for g in range(GROUPS):
        forward(g).wait_send()
    pltpu.make_async_copy(own.at[pl.ds(0, SELF)], own.at[pl.ds(0, SELF)], v_send).wait()
    pltpu.make_async_copy(qbuf.at[others], qbuf.at[others], q_send).wait()


def on_device(activations, out_grads, proj_in, proj_out, lengths, queries):
    any_space = pl.BlockSpec(memory_space=pl.ANY)
    dma = pltpu.SemaphoreType.DMA
    vmem = pltpu.VMEM
    slots = len(OFFSETS)
    return pl.pallas_call(
        kernel,
        out_shape=jax.ShapeDtypeStruct((32, 128), F32),
        in_specs=[any_space] * 6,
        out_specs=pl.BlockSpec(memory_space=pltpu.VMEM),
        scratch_shapes=[
            vmem((4, 1024, 1024), BF),
            vmem((4, 1024, 1024), BF),
            vmem((2, 2, 16, 1024), BF),
            vmem((2, 2, 1024, 128), BF),
            vmem((3, 256, 128), BF),
            vmem((3, 256, 128), BF),
            vmem((16, 256), BF),
            vmem((slots, 16, 256), BF),
            vmem((slots, 16, 256), BF),
            vmem((32, 16, 128), F32),
            pltpu.SMEM((32,), jnp.int32),
            vmem((4, 2, 256, 256), BF),
            dma((4, SUB, 2)),
            dma((2, 2)),
            dma,
            dma,
            dma((3,)),
            dma((3,)),
            dma,
            dma,
            dma,
            dma((GROUPS,)),
            dma((GROUPS,)),
            dma((GROUPS,)),
        ],
        compiler_params=pltpu.CompilerParams(
            collective_id=0, has_side_effects=True, vmem_limit_bytes=48 << 20
        ),
        name="influence",
    )(
        activations, out_grads, jnp.swapaxes(proj_in, 1, 2), jnp.swapaxes(proj_out, 1, 2), lengths, queries
    )


def solution(mesh):
    placed = (
        P(None, "dp", "tensor"),
        P(None, "dp", "tensor"),
        P(None, "tensor", None),
        P(None, "tensor", None),
        P("dp"),
        P("dp", "tensor"),
    )
    return jax.shard_map(
        on_device, mesh=mesh, in_specs=placed, out_specs=P("dp", "tensor"), check_vma=False
    )
```

time: 1090 us -> 34.8 us (0.03)
  the two profiles are of different devices: /device:TPU:0 before, /device:TPU:1 now
where the time goes in v1:
time: 34.8 us; the launch traced here: 34.6 us
  Pallas kernels  30.9 us (89%)
  local copies, waits for them, and re-layouts  3.64 us (10%)
    pallas_call x1, Pallas kernels, on_device(): pl.pallas_call(kernel, out_shape=jax.ShapeDtypeStruct((32, 128), F32), in...  30.9 us
    unnamed x9, local copies, waits for them, and re-layouts  3.64 us

profile of v1, /device:TPU:1, one launch (start us, length us, event | category | flops | bytes accessed | tf_op | source)
XLA Modules:
  0.0 34.6 jit_solution(15621927925502223478)
XLA Ops:
  0.0 0.0 copy-start
  0.0 0.8 %copy-done = bf16[2,1024,16]{1,2,0:T(8,128)(2,1)S(1)} copy-done((bf16[2,1024,16]{1,2,0:T(8,128)(2,1)S(1)}, bf16[2,1024,16]{1,2,0:T(8,128)(2,1)}, u32[]{:S(2)}) %copy-start) | copy-done | bytes 65560
  0.8 0.0 copy-start.1
  0.8 0.8 %copy-done.1 = bf16[2,1024,16]{1,2,0:T(8,128)(2,1)S(1)} copy-done((bf16[2,1024,16]{1,2,0:T(8,128)(2,1)S(1)}, bf16[2,1024,16]{1,2,0:T(8,128)(2,1)}, u32[]{:S(2)}) %copy-start.1) | copy-done | bytes 65560
  1.7 0.0 copy-start.2
  1.7 0.7 %copy-done.2 = f32[16,128]{1,0:T(8,128)S(1)} copy-done((f32[16,128]{1,0:T(8,128)S(1)}, f32[16,128]{1,0:T(8,128)}, u32[]{:S(2)}) %copy-start.2) | copy-done | bytes 8216
  2.4 0.0 copy-start.3
  2.4 0.7 %copy-done.3 = s32[32]{0:T(128)S(1)} copy-done((s32[32]{0:T(128)S(1)}, s32[32]{0:T(128)}, u32[]{:S(2)}) %copy-start.3) | copy-done | bytes 152
  3.0 30.9 %influence.1 = f32[32,128]{1,0:T(8,128)S(1)} custom-call(bf16[2,2048,1024]{2,1,0:T(8,128)(2,1)} %act.1, bf16[2,2048,1024]{2,1,0:T(8,128)(2,1)} %grad.1, bf16[2,16,1024]{2,1,0:T(8,128)(2,1)S(1)} %bitcast.2, bf16[2,16,1024]{2,1,0:T(8,128)(2,1)S(1)} %bitcast.3, s32[32]{0:T(128)S(1)} %copy-done.3, f32[16,128]{1,0:T(8,128)S(1)} %copy-done.2), custom_call_target="tpu_custom_call" | custom-call | tf_op jit(solution)/shard_map/influence/pallas_call | solution.py:242
  34.0 0.6 %copy.8 = f32[32,128]{1,0:T(8,128)} copy(f32[32,128]{1,0:T(8,128)S(1)} %influence.1) | data formatting | bytes 32768
Async XLA Ops:
  0.0 0.8 %copy-start = (bf16[2,1024,16]{1,2,0:T(8,128)(2,1)S(1)}, bf16[2,1024,16]{1,2,0:T(8,128)(2,1)}, u32[]{:S(2)}) copy-start(bf16[2,1024,16]{1,2,0:T(8,128)(2,1)} %param.8) | copy-start | bytes 196612
  0.8 0.8 %copy-start.1 = (bf16[2,1024,16]{1,2,0:T(8,128)(2,1)S(1)}, bf16[2,1024,16]{1,2,0:T(8,128)(2,1)}, u32[]{:S(2)}) copy-start(bf16[2,1024,16]{1,2,0:T(8,128)(2,1)} %param.9) | copy-start | bytes 196612
  1.7 0.7 %copy-start.2 = (f32[16,128]{1,0:T(8,128)S(1)}, f32[16,128]{1,0:T(8,128)}, u32[]{:S(2)}) copy-start(f32[16,128]{1,0:T(8,128)} %queries.1) | copy-start | bytes 24580
  2.4 0.7 %copy-start.3 = (s32[32]{0:T(128)S(1)}, s32[32]{0:T(128)}, u32[]{:S(2)}) copy-start(s32[32]{0:T(128)} %lengths.1) | copy-start | bytes 388

commit v2 on v1

v2 whole, which is shorter than its diff:
```python
import math

import jax
import jax.numpy as jnp
from jax import lax
from jax.experimental import pallas as pl
from jax.experimental.pallas import tpu as pltpu
from jax.sharding import PartitionSpec as P

ITERS = 4
DAMPING = 0.1
MESH = pl.DeviceIdType.MESH
BF = jnp.bfloat16
F32 = jnp.float32

OFFSETS = sorted(
    [(a, b, c) for a in range(4) for b in range(4) for c in range(4)],
    key=lambda o: -sum(min(v, 4 - v) for v in o),
)
SLOTS = len(OFFSETS)
SELF = SLOTS - 1
ACROSS = OFFSETS.index((0, 0, 2))
GROUPS = 4
PER_GROUP = SLOTS // GROUPS
SUB = 2


def split(v):
    hi = v.astype(BF)
    return hi, (v - hi.astype(F32)).astype(BF)


def nt_dot(a, b):
    return lax.dot_general(a, b, (((1,), (1,)), ((), ())), preferred_element_type=F32)


def tn_dot(a, b):
    return lax.dot_general(a, b, (((0,), (0,)), ((), ())), preferred_element_type=F32)


def kernel(
    act, grad, pin, pout, lengths, queries, out,
    abuf, gbuf, pbuf, send, part, acc, own, oth, qbuf, lens, p_hi, p_lo, gram, g_hi, sol, res, dirn, norm,
    in_sem, p_sem, q_sem, l_sem, rs_send, rs_recv, q_send, q_recv, v_send, v_recv, f_send, f_recv, plane_sem, all_sem,
):
    dp, tensor = lax.axis_index("dp"), lax.axis_index("tensor")
    x, y = lax.rem(dp // 2, 4), dp // 8
    zl = lax.rem(dp, 2)
    zh, core = tensor // 2, lax.rem(tensor, 2)
    z = zh * 2 + zl

    def chip(dx, dy, dz, flip=0):
        tx, ty, tz = lax.rem(x + dx, 4), lax.rem(y + dy, 4), lax.rem(z + dz, 4)
        return ((ty * 4 + tx) * 2 + lax.rem(tz, 2), (tz // 2) * 2 + lax.rem(core + flip, 2))

    sibling = chip(0, 0, 0, 1)
    step = 1024 // SUB

    def other_linear(k):
        return lax.rem((k + 1) // 2, 2)

    def far(k):
        return 1 - k // 2

    def load(k, s, which):
        linear = lax.rem(core + other_linear(k), 2)
        half = lax.rem(zh + far(k), 2)
        src, dst = ((act, abuf), (grad, gbuf))[which]
        return pltpu.make_async_copy(
            src.at[linear, pl.ds(pl.multiple_of(half * 1024 + s * step, step), step)],
            dst.at[k, pl.ds(pl.multiple_of(s * step, step), step)],
            in_sem.at[k, s, which],
        )

    def scatter(k):
        return pltpu.make_async_remote_copy(
            src_ref=send.at[k], dst_ref=part.at[k], send_sem=rs_send.at[k], recv_sem=rs_recv.at[k],
            device_id=chip(0, 0, 2 * far(k), other_linear(k)), device_id_type=MESH,
        )

    weights = [pltpu.make_async_copy(p, pbuf.at[io], p_sem.at[io]) for io, p in enumerate((pin, pout))]
    for c in weights:
        c.start()

    @pl.loop(0, 4 * SUB)
    def _(n):
        for which in range(2):
            load(n // SUB, lax.rem(n, SUB), which).start()

    len_copy = pltpu.make_async_copy(lengths, lens, l_sem)
    len_copy.start()
    q_y = lax.rem(y + 2 * core, 4)
    q_copy = pltpu.make_async_copy(queries, qbuf.at[q_y, zl, x], q_sem)
    q_copy.start()

    barrier = pltpu.get_barrier_semaphore()

    for t in (chip(0, 0, 2), chip(0, 0, 2, 1), sibling):
        pl.semaphore_signal(barrier, inc=1, device_id=t, device_id_type=MESH)
    for d in (1, 2, 3):
        for t in (chip(d, 0, 0), chip(0, d, 0)) + ((chip(0, 0, d),) if d != 2 else ()):
            pl.semaphore_signal(barrier, inc=1, device_id=t, device_id_type=MESH)

    def query_row(n):
        return pltpu.make_async_remote_copy(
            src_ref=qbuf.at[q_y, zl, x], dst_ref=qbuf.at[q_y, zl, x], send_sem=q_send.at[0], recv_sem=q_recv.at[0],
            device_id=chip(n, 0, 0), device_id_type=MESH,
        )

    def query_plane(n):
        ty, tl = lax.rem(y + lax.rem(n, 4), 4), lax.rem(zl + n // 4, 2)
        return pltpu.make_async_remote_copy(
            src_ref=qbuf.at[q_y, zl], dst_ref=qbuf.at[q_y, zl], send_sem=q_send.at[1], recv_sem=q_recv.at[1],
            device_id=((ty * 4 + x) * 2 + tl, tensor), device_id_type=MESH,
        )

    for c in weights:
        c.wait()

    @pl.loop(0, 4)
    def _(k):
        linear = lax.rem(core + other_linear(k), 2)

        for s in range(SUB):
            rows = pl.ds(s * step, step)
            for which, buf in enumerate((abuf, gbuf)):
                load(k, s, which).wait()
                acc[which * 16:which * 16 + 16, rows] = nt_dot(pbuf[which, linear], buf[k, rows])

        @pl.when(k == 0)
        def _():
            pl.semaphore_wait(barrier, 11)

        @pl.when(k < 3)
        def _():
            send[k] = acc[...].astype(BF)
            scatter(k).start()

        @pl.when(k == 0)
        def _():
            for d in (2, 1, 3):
                pl.semaphore_signal(plane_sem, inc=1, device_id=chip(0, d, 0), device_id_type=MESH)
            q_copy.wait()
            for n in (2, 1, 3):
                query_row(n).start()

        @pl.when(k == 1)
        def _():
            pl.semaphore_wait(plane_sem, 3)
            for d in (2, 1, 3):
                pl.semaphore_signal(all_sem, inc=1, device_id=chip(0, 0, d), device_id_type=MESH)

        @pl.when(k == 2)
        def _():
            pl.semaphore_wait(all_sem, 3)
            pltpu.make_async_copy(qbuf.at[0, 0, pl.ds(0, 3)], qbuf.at[0, 0, pl.ds(0, 3)], q_recv.at[0]).wait()

            @pl.loop(1, 8)
            def _(n):
                query_plane(n).start()

    len_copy.wait()
    seq = lax.broadcasted_iota(jnp.int32, (16, 1024), 0)
    token = lax.broadcasted_iota(jnp.int32, (16, 1024), 1) - 64 * seq
    row = seq[:, :128]
    limit = jnp.zeros((16, 128), jnp.int32)
    for s in range(16):
        limit = jnp.where(row == s, lens[zh * 16 + s], limit)
    limit = jnp.concatenate([limit] * 8, axis=1)
    live = jnp.where((token >= 0) & (token < limit), 1.0 / math.sqrt(64), 0.0).astype(BF)

    total = acc[...]
    for k in (2, 0, 1):
        scatter(k).wait_recv()
        total = total + part[k].astype(F32)
    acc[...] = total

    @pl.loop(0, 16)
    def _(a):
        prod = acc[pl.ds(16 + a, 1)] * acc[:16]
        hi, lo = split(prod)
        rows = pl.ds(pl.multiple_of(a * 16, 16), 16)
        p_hi[rows] = hi
        p_lo[rows] = lo

    own[SELF] = (nt_dot(live, p_hi[...]) + nt_dot(live, p_lo[...])).astype(BF)

    for k in range(SELF):
        pltpu.make_async_remote_copy(
            src_ref=own.at[SELF], dst_ref=own.at[k], send_sem=v_send, recv_sem=v_recv.at[k // PER_GROUP],
            device_id=chip(*OFFSETS[k]), device_id_type=MESH,
        ).start()

    def group(g):
        return pl.ds(g * PER_GROUP, PER_GROUP)

    def forward(g):
        return pltpu.make_async_remote_copy(
            src_ref=own.at[group(g)], dst_ref=oth.at[group(g)], send_sem=f_send.at[g], recv_sem=f_recv.at[g],
            device_id=sibling, device_id_type=MESH,
        )

    for g in range(GROUPS):
        got = pl.ds(g * PER_GROUP, min(PER_GROUP, SELF - g * PER_GROUP))
        pltpu.make_async_copy(own.at[got], own.at[got], v_recv.at[g]).wait()
        forward(g).start()

    gram[...] = jnp.zeros((512, 512), F32)

    @pl.loop(0, GROUPS)
    def _(g):
        forward(g).wait_recv()
        vecs = jnp.concatenate(
            [own[group(g)].reshape(256, 256), oth[group(g)].reshape(256, 256)], axis=1
        )
        gram[...] += tn_dot(vecs, vecs)

    g_hi[...] = (gram[...] * (1.0 / 1024)).astype(BF)

    rows = res.at[pl.ds(0, 448)]
    pltpu.make_async_copy(rows, rows, q_recv.at[1]).wait()
    start = jnp.concatenate(
        [qbuf[a, b, c] for a in range(4) for c in range(4) for b in range(2)], axis=0
    )
    res[...] = start
    dirn[...] = start
    sol[...] = jnp.zeros_like(start)
    norm[...] = jnp.sum(start * start, axis=0, keepdims=True)

    @pl.loop(0, ITERS)
    def _(it):
        direction = dirn[...]
        norm_now = norm[...]
        d_hi, d_lo = split(direction)
        wide = jnp.dot(g_hi[...], jnp.concatenate([d_hi, d_lo], axis=1), preferred_element_type=F32)
        image = wide[:, :128] + wide[:, 128:] + DAMPING * direction
        step_size = norm_now / jnp.sum(direction * image, axis=0, keepdims=True)
        sol[...] += step_size * direction

        @pl.when(it < ITERS - 1)
        def _():
            residual = res[...] - step_size * image
            norm_next = jnp.sum(residual * residual, axis=0, keepdims=True)
            res[...] = residual
            dirn[...] = residual + norm_next / norm_now * direction
            norm[...] = norm_next

    solution = sol[...].astype(BF)
    scale = 1.0 / math.sqrt(512)
    for slot, half in ((SELF, zh), (ACROSS, 1 - zh)):
        v = jnp.concatenate([own[slot], oth[slot]], axis=1)
        out[pl.ds(pl.multiple_of(half * 16, 16), 16)] = jnp.dot(v, solution, preferred_element_type=F32) * scale

    for k in range(3):
        scatter(k).wait_send()
    for g in range(GROUPS):
        forward(g).wait_send()
    pltpu.make_async_copy(own.at[pl.ds(0, SELF)], own.at[pl.ds(0, SELF)], v_send).wait()
    pltpu.make_async_copy(qbuf.at[0, 0, pl.ds(0, 3)], qbuf.at[0, 0, pl.ds(0, 3)], q_send.at[0]).wait()
    pltpu.make_async_copy(rows, rows, q_send.at[1]).wait()


def on_device(activations, out_grads, proj_in, proj_out, lengths, queries):
    any_space = pl.BlockSpec(memory_space=pl.ANY)
    dma = pltpu.SemaphoreType.DMA
    vmem = pltpu.VMEM
    return pl.pallas_call(
        kernel,
        out_shape=jax.ShapeDtypeStruct((32, 128), F32),
        in_specs=[any_space] * 6,
        out_specs=pl.BlockSpec(memory_space=pltpu.VMEM),
        scratch_shapes=[
            vmem((4, 1024, 1024), BF),
            vmem((4, 1024, 1024), BF),
            vmem((2, 2, 16, 1024), BF),
            vmem((3, 32, 1024), BF),
            vmem((3, 32, 1024), BF),
            vmem((32, 1024), F32),
            vmem((SLOTS, 16, 256), BF),
            vmem((SLOTS, 16, 256), BF),
            vmem((4, 2, 4, 16, 128), F32),
            pltpu.SMEM((32,), jnp.int32),
            vmem((256, 1024), BF),
            vmem((256, 1024), BF),
            vmem((512, 512), F32),
            vmem((512, 512), BF),
            vmem((512, 128), F32),
            vmem((512, 128), F32),
            vmem((512, 128), F32),
            vmem((1, 128), F32),
            dma((4, SUB, 2)),
            dma((2,)),
            dma,
            dma,
            dma((3,)),
            dma((3,)),
            dma((2,)),
            dma((2,)),
            dma,
            dma((GROUPS,)),
            dma((GROUPS,)),
            dma((GROUPS,)),
            pltpu.SemaphoreType.REGULAR,
            pltpu.SemaphoreType.REGULAR,
        ],
        compiler_params=pltpu.CompilerParams(
            collective_id=0, has_side_effects=True, vmem_limit_bytes=60 << 20
        ),
        name="influence",
    )(
        activations, out_grads, jnp.swapaxes(proj_in, 1, 2), jnp.swapaxes(proj_out, 1, 2), lengths, queries
    )


def solution(mesh):
    placed = (
        P(None, "dp", "tensor"),
        P(None, "dp", "tensor"),
        P(None, "tensor", None),
        P(None, "tensor", None),
        P("dp"),
        P("dp", "tensor"),
    )
    return jax.shard_map(
        on_device, mesh=mesh, in_specs=placed, out_specs=P("dp", "tensor"), check_vma=False
    )
```

time: 34.8 us -> 32.6 us (0.937)
  local copies, waits for them, and re-layouts: 3.64 us -> 1.32 us
    unnamed x9 -> x1, local copies, waits for them, and re-layouts: 3.64 us -> 1.32 us
where the time goes in v2:
time: 32.6 us; the launch traced here: 32.4 us
  Pallas kernels  31.1 us (95%)
  local copies, waits for them, and re-layouts  1.32 us (4%)
    pallas_call x1, Pallas kernels, on_device(): pl.pallas_call(kernel, out_shape=jax.ShapeDtypeStruct((32, 128), F32), in...  31.1 us
    unnamed x1, local copies, waits for them, and re-layouts  1.32 us

profile of v2, /device:TPU:1, one launch (start us, length us, event | category | flops | bytes accessed | tf_op | source)
XLA Modules:
  0.0 32.4 jit_solution(16241363320296117088)
XLA Ops:
  0.0 31.1 %influence.1 = f32[32,128]{1,0:T(8,128)} custom-call(bf16[2,2048,1024]{2,1,0:T(8,128)(2,1)} %act.1, bf16[2,2048,1024]{2,1,0:T(8,128)(2,1)} %grad.1, bf16[2,16,1024]{2,1,0:T(8,128)(2,1)} %bitcast.2, bf16[2,16,1024]{2,1,0:T(8,128)(2,1)} %bitcast.3, s32[32]{0:T(128)} %lengths.1, f32[16,128]{1,0:T(8,128)} %queries.1), custom_call_target="tpu_custom_call" | custom-call | tf_op jit(solution)/shard_map/influence/pallas_call | solution.py:267
  31.1 1.3 %copy.8 = f32[32,128]{1,0:T(8,128)} copy(f32[32,128]{1,0:T(8,128)} %influence.1) | data formatting | bytes 32768

commit v3 on v2

--- a/solution.py
+++ b/solution.py
@@ -85,7 +85,7 @@
     @pl.loop(0, 4 * SUB)
     def _(n):
         for which in range(2):
-            load(n // SUB, lax.rem(n, SUB), which).start()
+            load(n // SUB, lax.rem(n, SUB), which).start(priority=which)
 
     len_copy = pltpu.make_async_copy(lengths, lens, l_sem)
     len_copy.start()
@@ -266,7 +266,7 @@
     vmem = pltpu.VMEM
     return pl.pallas_call(
         kernel,
-        out_shape=jax.ShapeDtypeStruct((32, 128), F32),
+        out_shape=pltpu.VMEM((32, 128), F32),
         in_specs=[any_space] * 6,
         out_specs=pl.BlockSpec(memory_space=pltpu.VMEM),
         scratch_shapes=[

time: 32.6 us -> 30.6 us (0.939)
  Pallas kernels: 31.1 us -> 29.9 us
  local copies, waits for them, and re-layouts: 1.32 us -> 0.61 us
    pallas_call x1, Pallas kernels: 31.1 us -> 29.9 us  [on_device(): pl.pallas_call(kernel, out_shape=pltpu.VMEM((32, 128), F32), in_specs=[an...]
    unnamed x1, local copies, waits for them, and re-layouts: 1.32 us -> 0.61 us
where the time goes in v3:
time: 30.6 us; the launch traced here: 30.5 us
  Pallas kernels  29.9 us (98%)
  local copies, waits for them, and re-layouts  0.61 us (2%)
    pallas_call x1, Pallas kernels, on_device(): pl.pallas_call(kernel, out_shape=pltpu.VMEM((32, 128), F32), in_specs=[an...  29.9 us

profile of v3, /device:TPU:1, one launch (start us, length us, event | category | flops | bytes accessed | tf_op | source)
XLA Modules:
  0.0 30.5 jit_solution(14127699833842031856)
XLA Ops:
  0.0 29.9 %influence.1 = f32[32,128]{1,0:T(8,128)S(1)} custom-call(bf16[2,2048,1024]{2,1,0:T(8,128)(2,1)} %act.1, bf16[2,2048,1024]{2,1,0:T(8,128)(2,1)} %grad.1, bf16[2,16,1024]{2,1,0:T(8,128)(2,1)} %bitcast.2, bf16[2,16,1024]{2,1,0:T(8,128)(2,1)} %bitcast.3, s32[32]{0:T(128)} %lengths.1, f32[16,128]{1,0:T(8,128)} %queries.1), custom_call_target="tpu_custom_call" | custom-call | tf_op jit(solution)/shard_map/influence/pallas_call | solution.py:267
  29.9 0.6 %copy.8 = f32[32,128]{1,0:T(8,128)} copy(f32[32,128]{1,0:T(8,128)S(1)} %influence.1) | data formatting | bytes 32768

commit v4 on v3

--- a/solution.py
+++ b/solution.py
@@ -85,7 +85,7 @@
     @pl.loop(0, 4 * SUB)
     def _(n):
         for which in range(2):
-            load(n // SUB, lax.rem(n, SUB), which).start(priority=which)
+            load(n // SUB, lax.rem(n, SUB), which).start(priority=1)
 
     len_copy = pltpu.make_async_copy(lengths, lens, l_sem)
     len_copy.start()

time: 30.6 us -> 28.5 us (0.931)
  Pallas kernels: 29.9 us -> 27.8 us
    pallas_call x1, Pallas kernels: 29.9 us -> 27.8 us  [on_device(): pl.pallas_call(kernel, out_shape=pltpu.VMEM((32, 128), F32), in_specs=[an...]
where the time goes in v4:
time: 28.5 us; the launch traced here: 28.4 us
  Pallas kernels  27.8 us (98%)
  local copies, waits for them, and re-layouts  0.61 us (2%)
    pallas_call x1, Pallas kernels, on_device(): pl.pallas_call(kernel, out_shape=pltpu.VMEM((32, 128), F32), in_specs=[an...  27.8 us
    unnamed x1, local copies, waits for them, and re-layouts  0.61 us

profile of v4, /device:TPU:1, one launch (start us, length us, event | category | flops | bytes accessed | tf_op | source)
XLA Modules:
  0.0 28.4 jit_solution(16484674123357947566)
XLA Ops:
  0.0 27.8 %influence.1 = f32[32,128]{1,0:T(8,128)S(1)} custom-call(bf16[2,2048,1024]{2,1,0:T(8,128)(2,1)} %act.1, bf16[2,2048,1024]{2,1,0:T(8,128)(2,1)} %grad.1, bf16[2,16,1024]{2,1,0:T(8,128)(2,1)} %bitcast.2, bf16[2,16,1024]{2,1,0:T(8,128)(2,1)} %bitcast.3, s32[32]{0:T(128)} %lengths.1, f32[16,128]{1,0:T(8,128)} %queries.1), custom_call_target="tpu_custom_call" | custom-call | tf_op jit(solution)/shard_map/influence/pallas_call | solution.py:267
  27.8 0.6 %copy.8 = f32[32,128]{1,0:T(8,128)} copy(f32[32,128]{1,0:T(8,128)S(1)} %influence.1) | data formatting | bytes 32768

commit v5 on v4

--- a/solution.py
+++ b/solution.py
@@ -153,11 +153,6 @@
         @pl.when(k == 2)
         def _():
             pl.semaphore_wait(all_sem, 3)
-            pltpu.make_async_copy(qbuf.at[0, 0, pl.ds(0, 3)], qbuf.at[0, 0, pl.ds(0, 3)], q_recv.at[0]).wait()
-
-            @pl.loop(1, 8)
-            def _(n):
-                query_plane(n).start()
 
     len_copy.wait()
     seq = lax.broadcasted_iota(jnp.int32, (16, 1024), 0)
@@ -190,6 +185,12 @@
             src_ref=own.at[SELF], dst_ref=own.at[k], send_sem=v_send, recv_sem=v_recv.at[k // PER_GROUP],
             device_id=chip(*OFFSETS[k]), device_id_type=MESH,
         ).start()
+
+    pltpu.make_async_copy(qbuf.at[0, 0, pl.ds(0, 3)], qbuf.at[0, 0, pl.ds(0, 3)], q_recv.at[0]).wait()
+
+    @pl.loop(1, 8)
+    def _(n):
+        query_plane(n).start()
 
     def group(g):
         return pl.ds(g * PER_GROUP, PER_GROUP)

time: 28.5 us -> 28.4 us (level)
  no operation moved by 1% of the time
where the time goes in v5:
time: 28.4 us; the launch traced here: 28.3 us
  Pallas kernels  27.7 us (98%)
  local copies, waits for them, and re-layouts  0.61 us (2%)
    pallas_call x1, Pallas kernels, on_device(): pl.pallas_call(kernel, out_shape=pltpu.VMEM((32, 128), F32), in_specs=[an...  27.7 us
    unnamed x1, local copies, waits for them, and re-layouts  0.61 us

profile of v5, /device:TPU:1, one launch (start us, length us, event | category | flops | bytes accessed | tf_op | source)
XLA Modules:
  0.0 28.3 jit_solution(6454393589473496101)
XLA Ops:
  0.0 27.7 %influence.1 = f32[32,128]{1,0:T(8,128)S(1)} custom-call(bf16[2,2048,1024]{2,1,0:T(8,128)(2,1)} %act.1, bf16[2,2048,1024]{2,1,0:T(8,128)(2,1)} %grad.1, bf16[2,16,1024]{2,1,0:T(8,128)(2,1)} %bitcast.2, bf16[2,16,1024]{2,1,0:T(8,128)(2,1)} %bitcast.3, s32[32]{0:T(128)} %lengths.1, f32[16,128]{1,0:T(8,128)} %queries.1), custom_call_target="tpu_custom_call" | custom-call | tf_op jit(solution)/shard_map/influence/pallas_call | solution.py:268
  27.7 0.6 %copy.8 = f32[32,128]{1,0:T(8,128)} copy(f32[32,128]{1,0:T(8,128)S(1)} %influence.1) | data formatting | bytes 32768
